TPU v7x, 32 devices: a whole 2x2x4 slice. The times are simulated.
32 devices in a mesh: tower: 2 (over core), rows: 16 (over z, y, x).
Axes of the slice: x: 2, y: 2, z: 4, core: 2. Of those that a mesh axis runs over, the one named last changes fastest.
Arguments:
- tokens: bfloat16 [2, 32, 512, 512], P('tower', 'rows'), may hold values from -9 to 9
- segment_ids: int32 [2, 32, 512], P('tower', 'rows'), may hold values from 0 to 8, never falling along the last dimension, each value on 1 to 128 neighbouring positions
- positives: int32 [256], P('rows'), may hold values from 0 to 255, each once
- attention_gain: float32 [512], replicated, may hold values from 0.5 to 1.5
- query_weight: bfloat16 [512, 512], replicated, may hold values from -0.0625 to 0.0625
- key_weight: bfloat16 [512, 512], replicated, may hold values from -0.25 to 0.25
- value_weight: bfloat16 [512, 512], replicated, may hold values from -0.25 to 0.25
- output_weight: bfloat16 [512, 512], replicated, may hold values from -1 to 1
- position_table: float32 [32, 8], replicated, may hold values from -3 to 3
- feedforward_gain: float32 [512], replicated, may hold values from 0.5 to 1.5
- inner_weight: bfloat16 [512, 2048], replicated, may hold values from -0.25 to 0.25
- outer_weight: bfloat16 [2048, 512], replicated, may hold values from -0.1875 to 0.1875
Outputs:
- layer_output: bfloat16 [2, 32, 512, 512], P('tower', 'rows')
- token_grad: bfloat16 [2, 32, 512, 512], P('tower', 'rows')
- attention_gain_grad: float32 [512], replicated
- query_grad: float32 [512, 512], replicated
- key_grad: float32 [512, 512], replicated
- value_grad: float32 [512, 512], replicated
- output_grad: float32 [512, 512], replicated
- position_grad: float32 [32, 8], replicated
- feedforward_gain_grad: float32 [512], replicated
- inner_grad: float32 [512, 2048], replicated
- outer_grad: float32 [2048, 512], replicated
- contrastive_loss: float32 [], replicated
- root_mean_squares: float32 [3], replicated
Inputs may be any that keep to these rules, and one draw needn't show every extreme that they name: `segment_ids`: within each row of 512 tokens the numbers never fall; 0 to 7 are the row's items and 8 marks the padding at its end; every number, padding included, covers 1 to 128 tokens. positives[m] is the document item paired with query item m; every document item occurs once.
All inputs are finite; a program needn't handle non-finite values.
Results may differ from a plain program's by a relative error of at most 0.028.
The roundings to bfloat16 on the way count: a program that leaves them out, or rounds other values in their place, can miss the bound.
Values sent between devices are 32-bit elements; how exact they have to be, the bound alone decides.
A program may use at most 320 MiB of HBM per device.

v0:
```python
import math
import jax
import jax.numpy as jnp
import numpy as np
from jax import lax
from jax.sharding import PartitionSpec as P

MAX_DIST = 128
ITEMS_ROW = 8
EPSILON = 1e-06
SOFTMAX_TEMP = 0.01
LOSS_SCALE = 65536.0
MATMUL_PRECISION = lax.Precision.HIGHEST


def from_partner(value, axis, apart):
    mask = 2**apart
    pairs = [(source, source ^ mask) for source in range(lax.axis_size(axis))]
    return lax.ppermute(value, axis, pairs)


def bucket_table(length, bucket_count, far_limit):
    half_count = bucket_count // 2
    exact_count = half_count // 2
    entries = []
    for offset in range(1 - length, length):
        distance = abs(offset)
        if distance < exact_count:
            within = distance
        else:
            within = exact_count + int(
                math.log(distance / exact_count)
                / math.log(far_limit / exact_count)
                * (half_count - exact_count)
            )
            within = min(within, half_count - 1)
        entries.append(within + (half_count if offset > 0 else 0))
    by_offset = np.array(entries, dtype=np.int32)
    index_grid = np.arange(length)[None, :] - np.arange(length)[:, None] + length - 1
    return (by_offset, by_offset[index_grid])


def contract_rows(left_side, right_side):
    return lax.dot_general(
        left_side, right_side, (((0,), (0,)), ((), ())), preferred_element_type=jnp.float32
    )


def times_transpose(left_side, right_side):
    return lax.dot_general(
        left_side, right_side, (((1,), (1,)), ((), ())), preferred_element_type=jnp.float32
    )


def norm_scale(values):
    return lax.rsqrt(jnp.mean(values * values, axis=1, keepdims=True) + EPSILON)


def norm_back(grad_normed, values, scale, gain):
    gained = grad_normed * gain
    return scale * (
        gained - values * scale * scale * jnp.mean(gained * values, axis=1, keepdims=True)
    )


def row_scores(query_part, key_part, segment_row, position_bias, head_count):
    length = query_part.shape[0]
    query_heads = query_part.reshape(length, head_count, -1)
    key_heads = key_part.reshape(length, head_count, -1)
    scores = (
        jnp.einsum("qhd,khd->hqk", query_heads, key_heads, preferred_element_type=jnp.float32)
        + position_bias
    )
    same_item = segment_row[:, None] == segment_row[None, :]
    return jnp.where(same_item[None], scores, -1e30)


def diagonal_sums(square):
    head_count = square.shape[0]
    length = square.shape[1]
    flipped = square[:, :, ::-1]
    padded = jnp.pad(flipped, ((0, 0), (0, 0), (0, length)))
    sheared = padded.reshape(head_count, 2 * length * length)[:, : length * (2 * length - 1)]
    sheared = sheared.reshape(head_count, length, 2 * length - 1)
    return jnp.sum(sheared, axis=1)[:, ::-1]


def shards(
    tokens,
    segment_ids,
    positives,
    attention_gain,
    query_weight,
    key_weight,
    value_weight,
    output_weight,
    position_table,
    feedforward_gain,
    inner_weight,
    outer_weight,
):
    row_count = tokens.shape[1]
    length = tokens.shape[2]
    model_width = tokens.shape[3]
    head_count = position_table.shape[1]
    inner_width = query_weight.shape[1]
    head_size = inner_width // head_count
    token_count = row_count * length
    by_offset, bucket_index = bucket_table(length, position_table.shape[0], MAX_DIST)
    position_bias = jnp.take(position_table.T, jnp.asarray(bucket_index), axis=1)
    inputs = tokens.reshape(token_count, model_width).astype(jnp.float32)
    segments = segment_ids.reshape(row_count, length)
    scale_one = norm_scale(inputs)
    normed_one = (inputs * scale_one * attention_gain).astype(jnp.bfloat16)
    query_rows = jnp.dot(normed_one, query_weight, preferred_element_type=jnp.float32).astype(
        jnp.bfloat16
    )
    key_rows = jnp.dot(normed_one, key_weight, preferred_element_type=jnp.float32).astype(
        jnp.bfloat16
    )
    value_rows = jnp.dot(normed_one, value_weight, preferred_element_type=jnp.float32).astype(
        jnp.bfloat16
    )
    query_blocks = query_rows.reshape(row_count, length, inner_width)
    key_blocks = key_rows.reshape(row_count, length, inner_width)
    value_blocks = value_rows.reshape(row_count, length, inner_width)

    def attend(packed):
        query_part, key_part, value_part, segment_row = packed
        scores = row_scores(query_part, key_part, segment_row, position_bias, head_count)
        highest = jnp.max(scores, axis=2, keepdims=True)
        exp_scores = jnp.exp(scores - highest)
        exp_total = jnp.sum(exp_scores, axis=2, keepdims=True)
        attention_probs = (exp_scores / exp_total).astype(jnp.bfloat16)
        value_heads = value_part.reshape(length, head_count, head_size)
        mixed_heads = jnp.einsum(
            "hqk,khd->qhd", attention_probs, value_heads, preferred_element_type=jnp.float32
        )
        return (
            mixed_heads.reshape(length, inner_width).astype(jnp.bfloat16),
            (highest + jnp.log(exp_total))[:, :, 0],
        )

    mixed_blocks, log_totals = lax.map(attend, (query_blocks, key_blocks, value_blocks, segments))
    mixed_rows = mixed_blocks.reshape(token_count, inner_width)
    branch_one = jnp.dot(mixed_rows, output_weight, preferred_element_type=jnp.float32)
    middle = inputs + branch_one
    scale_two = norm_scale(middle)
    normed_two = (middle * scale_two * feedforward_gain).astype(jnp.bfloat16)
    hidden = jax.nn.relu(
        jnp.dot(normed_two, inner_weight, preferred_element_type=jnp.float32)
    ).astype(jnp.bfloat16)
    branch_two = jnp.dot(hidden, outer_weight, preferred_element_type=jnp.float32)
    result = middle + branch_two
    valid_mask = (segments < ITEMS_ROW).astype(jnp.float32).reshape(token_count, 1)
    stat_terms = jnp.stack(
        [
            jnp.sum(valid_mask * result * result),
            jnp.sum(valid_mask * branch_one * branch_one),
            jnp.sum(valid_mask * branch_two * branch_two),
            jnp.sum(valid_mask),
        ]
    )
    stat_totals = lax.psum(stat_terms, ("tower", "rows"))
    member = (segments[:, None, :] == jnp.arange(ITEMS_ROW)[None, :, None]).astype(jnp.float32)
    item_sizes = jnp.sum(member, axis=2, keepdims=True)
    result_blocks = result.reshape(row_count, length, model_width)
    pooled = (
        jnp.einsum("ris,rsd->rid", member, result_blocks, precision=MATMUL_PRECISION) / item_sizes
    )
    items_here = row_count * ITEMS_ROW
    pooled = pooled.reshape(items_here, model_width)
    inverse_norm = lax.rsqrt(jnp.sum(pooled * pooled, axis=1, keepdims=True) + EPSILON)
    embedded_tokens = pooled * inverse_norm
    tower_index = lax.axis_index("tower")
    is_query = tower_index == 0
    partner = from_partner(embedded_tokens, "tower", 0)
    query_vectors = jnp.where(is_query, embedded_tokens, partner)
    document_vectors = jnp.where(is_query, partner, embedded_tokens)
    gathered_documents = lax.all_gather(document_vectors, "rows", axis=0, tiled=True)
    item_total = gathered_documents.shape[0]
    half_items = items_here // 2
    my_queries = lax.dynamic_slice_in_dim(query_vectors, tower_index * half_items, half_items, 0)
    my_targets = lax.dynamic_slice_in_dim(positives, tower_index * half_items, half_items, 0)
    similarity_scores = (
        lax.dot_general(
            my_queries,
            gathered_documents,
            (((1,), (1,)), ((), ())),
            precision=MATMUL_PRECISION,
            preferred_element_type=jnp.float32,
        )
        / SOFTMAX_TEMP
    )
    highest = jnp.max(similarity_scores, axis=1, keepdims=True)
    exp_logits = jnp.exp(similarity_scores - highest)
    exp_total = jnp.sum(exp_logits, axis=1, keepdims=True)
    log_total = highest[:, 0] + jnp.log(exp_total[:, 0])
    is_target = jnp.arange(item_total)[None, :] == my_targets[:, None]
    target = jnp.sum(jnp.where(is_target, similarity_scores, 0.0), axis=1)
    loss_part = jnp.sum(log_total - target)
    similarity_gradient = (exp_logits / exp_total - is_target.astype(jnp.float32)) * (
        LOSS_SCALE / item_total
    )
    local_gradient = (
        jnp.dot(similarity_gradient, gathered_documents, precision=MATMUL_PRECISION) / SOFTMAX_TEMP
    )
    grad_documents = lax.psum_scatter(
        lax.dot_general(
            similarity_gradient,
            my_queries,
            (((0,), (0,)), ((), ())),
            precision=MATMUL_PRECISION,
            preferred_element_type=jnp.float32,
        )
        / SOFTMAX_TEMP,
        "rows",
        scatter_dimension=0,
        tiled=True,
    )
    partner_mine, partner_documents = from_partner((local_gradient, grad_documents), "tower", 0)
    query_side = jnp.where(
        is_query,
        jnp.concatenate([local_gradient, partner_mine], 0),
        jnp.concatenate([partner_mine, local_gradient], 0),
    )
    own_grad = jnp.where(is_query, query_side, grad_documents + partner_documents)
    inner_along = jnp.sum(own_grad * embedded_tokens, axis=1, keepdims=True)
    grad_pooled = inverse_norm * (own_grad - embedded_tokens * inner_along)
    per_token = grad_pooled.reshape(row_count, ITEMS_ROW, model_width) / item_sizes
    grad_result = jnp.einsum("ris,rid->rsd", member, per_token, precision=MATMUL_PRECISION).reshape(
        token_count, model_width
    )
    grad_branch_two = grad_result.astype(jnp.bfloat16)
    outer_grad = contract_rows(hidden, grad_branch_two)
    grad_hidden = times_transpose(grad_branch_two, outer_weight)
    grad_pre = jnp.where(hidden > 0, grad_hidden, 0.0).astype(jnp.bfloat16)
    inner_grad = contract_rows(normed_two, grad_pre)
    grad_normed_two = times_transpose(grad_pre, inner_weight)
    feedforward_gain_grad = jnp.sum(grad_normed_two * middle * scale_two, axis=0)
    grad_middle = grad_result + norm_back(grad_normed_two, middle, scale_two, feedforward_gain)
    grad_branch_one = grad_middle.astype(jnp.bfloat16)
    output_grad = contract_rows(mixed_rows, grad_branch_one)
    grad_mixed = times_transpose(grad_branch_one, output_weight).astype(jnp.bfloat16)
    grad_mixed_blocks = grad_mixed.reshape(row_count, length, inner_width)

    def attend_back(running, packed):
        query_part, key_part, value_part, segment_row, row_log_total, grad_part = packed
        scores = row_scores(query_part, key_part, segment_row, position_bias, head_count)
        attention_probs = jnp.exp(scores - row_log_total[:, :, None])
        query_heads = query_part.reshape(length, head_count, head_size)
        key_heads = key_part.reshape(length, head_count, head_size)
        value_heads = value_part.reshape(length, head_count, head_size)
        grad_heads = grad_part.reshape(length, head_count, head_size)
        grad_value = jnp.einsum(
            "hqk,qhd->khd",
            attention_probs.astype(jnp.bfloat16),
            grad_heads,
            preferred_element_type=jnp.float32,
        )
        grad_probs = jnp.einsum(
            "qhd,khd->hqk", grad_heads, value_heads, preferred_element_type=jnp.float32
        )
        row_dot = jnp.sum(attention_probs * grad_probs, axis=2, keepdims=True)
        grad_scores = (attention_probs * (grad_probs - row_dot)).astype(jnp.bfloat16)
        grad_query = jnp.einsum(
            "hqk,khd->qhd", grad_scores, key_heads, preferred_element_type=jnp.float32
        )
        grad_key = jnp.einsum(
            "hqk,qhd->khd", grad_scores, query_heads, preferred_element_type=jnp.float32
        )
        outputs = (
            grad_query.reshape(length, inner_width).astype(jnp.bfloat16),
            grad_key.reshape(length, inner_width).astype(jnp.bfloat16),
            grad_value.reshape(length, inner_width).astype(jnp.bfloat16),
        )
        return (running + grad_scores.astype(jnp.float32), outputs)

    score_sum, grad_rows = lax.scan(
        attend_back,
        jnp.zeros((head_count, length, length), jnp.float32),
        (query_blocks, key_blocks, value_blocks, segments, log_totals, grad_mixed_blocks),
    )
    grad_queries = grad_rows[0].reshape(token_count, inner_width)
    grad_keys = grad_rows[1].reshape(token_count, inner_width)
    grad_values = grad_rows[2].reshape(token_count, inner_width)
    query_grad = contract_rows(normed_one, grad_queries)
    key_grad = contract_rows(normed_one, grad_keys)
    value_grad = contract_rows(normed_one, grad_values)
    grad_normed_one = (
        times_transpose(grad_queries, query_weight)
        + times_transpose(grad_keys, key_weight)
        + times_transpose(grad_values, value_weight)
    )
    attention_gain_grad = jnp.sum(grad_normed_one * inputs * scale_one, axis=0)
    token_grad = grad_middle + norm_back(grad_normed_one, inputs, scale_one, attention_gain)
    offset_onehot = jnp.asarray(
        (by_offset[:, None] == np.arange(position_table.shape[0])[None, :]).astype(np.float32)
    )
    position_grad = jnp.dot(diagonal_sums(score_sum), offset_onehot, precision=MATMUL_PRECISION).T
    closing_terms = loss_part[None]
    summed = lax.psum(
        (
            attention_gain_grad,
            query_grad,
            key_grad,
            value_grad,
            output_grad,
            position_grad,
            feedforward_gain_grad,
            inner_grad,
            outer_grad,
            closing_terms,
        ),
        ("tower", "rows"),
    )
    (
        attention_gain_grad,
        query_grad,
        key_grad,
        value_grad,
        output_grad,
        position_grad,
        feedforward_gain_grad,
        inner_grad,
        outer_grad,
        closing_totals,
    ) = summed
    contrastive_loss = closing_totals[0] / item_total
    root_mean_squares = jnp.sqrt(stat_totals[:3] / (stat_totals[3] * model_width))
    block_shape = (1, row_count, length, model_width)
    return (
        result.reshape(block_shape).astype(jnp.bfloat16),
        token_grad.reshape(block_shape).astype(jnp.bfloat16),
        attention_gain_grad,
        query_grad,
        key_grad,
        value_grad,
        output_grad,
        position_grad,
        feedforward_gain_grad,
        inner_grad,
        outer_grad,
        contrastive_loss,
        root_mean_squares,
    )


def solution(mesh):
    return jax.shard_map(
        shards,
        mesh=mesh,
        in_specs=(
            P("tower", "rows", None, None),
            P("tower", "rows", None),
            P("rows"),
            P(),
            P(),
            P(),
            P(),
            P(),
            P(),
            P(),
            P(),
            P(),
        ),
        out_specs=(
            P("tower", "rows", None, None),
            P("tower", "rows", None, None),
            P(),
            P(),
            P(),
            P(),
            P(),
            P(),
            P(),
            P(),
            P(),
            P(),
            P(),
        ),
        check_vma=False,
    )
```

profile of v0, /device:TPU:0, one launch (start us, length us, event | category | flops | bytes accessed | tf_op | source)
XLA Modules:
  0.0 1486.5 jit_solution(8252469070416313084)
XLA Ops:
  26.5 865.7 %gather_fusion = f32[262144,8]{1,0:T(8,128)} fusion(f32[8,32]{0,1:T(8,128)S(1)} %bitcast.203, s32[262144]{0:T(1024)S(1)} %broadcast_clamp_fusion), kind=kCustom, calls=%fused_computation | custom fusion | bytes 17825792 | tf_op jit(solution)/shard_map/jit(_take)/gather | solution.py:110
  892.2 70.9 %copy.45 = f32[512,512,8]{0,1,2:T(8,128)} copy(f32[512,512,8]{2,1,0:T(8,128)} %bitcast.13) | data formatting | bytes 16777216 | tf_op jit(solution)/shard_map/jit(_take)/gather | solution.py:110
  964.2 22.9 %while.29 = (s32[]{:T(128)}, bf16[2,512,512]{2,1,0:T(8,128)(2,1)}, f32[2,8,512]{2,1,0:T(8,128)S(1)}, bf16[2,512,512]{1,2,0:T(8,128)(2,1)}, s32[2,512]{1,0:T(2,12...) while((s32[]{:T(128)}, bf16[2,512,512]{2,1,0:T(8,128)(2,1)}, ...), condition=%wide.region_4.5_spmd, body=%wide.region_1.0_spmd.sunk | while | flops 554168320 | bytes 41556588 | solution.py:144
  965.7 5.0 fusion.126
  977.1 5.0 fusion.126
  992.1 3.4 fusion.8
  999.4 45.4 %all_gather.3 = f32[256,512]{1,0:T(8,128)S(1)} all-gather(f32[16,512]{1,0:T(8,128)S(1)} %broadcast_select_fusion), channel_id=1, replica_groups=mesh['tower'=2,'rows'=16] {'rows'}, dimensions={0}, use_global_device_ids=true | all-gather | bytes 557056 | tf_op jit(solution)/shard_map/all_gather | solution.py:180
  1050.2 70.9 %reduce-scatter.2.cloned.1.call-done = f32[16,512]{1,0:T(8,128)} async-done(((f32[256,512]{1,0:T(8,128)}), f32[16,512]{1,0:T(8,128)}) %reduce-scatter.2.cloned.1.call-update) | async-done | bytes 32784 | tf_op jit(solution)/shard_map/reduce_scatter | solution.py:208
  1125.4 4.7 select_convert_fusion
  1130.2 4.5 fusion.56
  1137.8 4.6 fusion.44
  1150.7 74.2 %while.30 = (s32[]{:T(128)}, f32[8,512,512]{1,2,0:T(8,128)}, bf16[2,512,512]{2,1,0:T(8,128)(2,1)}, bf16[2,512,512]{2,1,0:T(8,128)(2,1)}, bf16[2,512,512]{2,1,0:T...) while((s32[]{:T(128)}, f32[8,512,512]{1,2,0:T(8,128)}, ...), condition=%wide.region_15.16_spmd.clone, body=%wide.region_13.15_spmd.clone.sunk | while | flops 1368387584 | bytes 197745472 | solution.py:279
  1153.4 3.4 constant_dynamic-slice_fusion.22
  1159.0 5.0 multiply_reduce_fusion.7
  1164.0 9.8 select_add_fusion.2
  1175.9 4.8 fusion.140
  1188.9 3.4 constant_dynamic-slice_fusion.22
  1194.5 5.0 multiply_reduce_fusion.7
  1199.5 13.0 select_add_fusion.2
  1214.6 4.8 fusion.140
  1225.0 3.4 fusion.53
  1238.3 64.2 %rev.6 = f32[8,512,512]{1,2,0:T(8,128)} reverse(f32[8,512,512]{1,2,0:T(8,128)} %get-tuple-element.126), dimensions={2} | reverse | bytes 16777216 | tf_op jit(solution)/shard_map/rev | solution.py:81
  1302.6 9.6 copy.71
  1312.2 11.6 pad_bitcast_fusion
  1323.9 15.4 %copy.73 = f32[1,8,512,1024]{3,1,2,0:T(8,128)S(1)} copy(f32[1,8,512,1024]{3,2,1,0:T(8,128)} %pad_bitcast_fusion) | data formatting | bytes 33554432
  1339.3 6.0 slice.14
  1345.3 13.0 reshape.408
  1358.2 17.5 %reshape.392 = f32[8,512,1023]{2,1,0:T(8,128)} reshape(f32[4190208]{0:T(1024)} %reshape.408) | data formatting | bytes 33521664 | tf_op jit(solution)/shard_map/reshape | solution.py:84
  1375.8 7.4 reduce_sum.180
  1389.2 37.9 %all-reduce.1 = (f32[512]{0:T(512)}, f32[32,8]{0,1:T(8,128)}, f32[512]{0:T(512)}, f32[1]{0:T(128)}, f32[4]{0:T(128)S(1)}) all-reduce(f32[512]{0:T(512)S(1)} %get-tuple-element.208, f32[32,8]{0,1:T(8,128)S(1)} %fusion.48, f32[512]{0:T(512)S(1)} %copy-done.46, f32[1]{0:T(128)} %bitcast.27, ...), channel_id=1, replica_groups=mesh['tower'=2,'rows'=16] {'tower','rows'}, use_global_device_ids=true, to_apply=%region_18.19 | all-reduce | flops 1285 | bytes 10280 | tf_op jit(solution)/shard_map/psum | solution.py:302
  1429.5 4.1 fusion.18
  1433.6 32.4 %all-reduce.5.cloned.1.call-done = (f32[512,512]{1,0:T(8,128)}, f32[512,512]{1,0:T(8,128)}, f32[512,512]{1,0:T(8,128)}, f32[512,512]{1,0:T(8,128)}, f32[512,2048]{1,0:T(8,128)}, /*index=5*/f32[2048,512]{1,0:T(8,128)}) async-done(((f32[512,512]{1,0:T(8,128)}, f32[512,512]{1,0:T(8,128)}, f32[512,512]{1,0:T(8,128)}, f32[512,512]{1,0:T(8,128)}, f32[512,2048]{1,0:T(8,128)}, /*index=5*/f32[2048,512]{1,0:T(8,128)}), ...) | async-done | bytes 12582928 | tf_op jit(solution)/shard_map/psum | solution.py:302
  (235 shorter events, 117.2 us)
Async XLA Ops:
  7.2 982.5 %copy-start = (bf16[512,2048]{1,0:T(8,128)(2,1)S(1)}, bf16[512,2048]{1,0:T(8,128)(2,1)}, u32[]{:S(2)}) copy-start(bf16[512,2048]{1,0:T(8,128)(2,1)} %param.28) | copy-start | bytes 6291460
  7.2 1114.0 %reduce-scatter.2.cloned.1.call-start = ((), (), s32[]{:S(2)}) async-start(), calls=%async_computation.1 | async-start | bytes 557056 | tf_op jit(solution)/shard_map/reduce_scatter | solution.py:208
  7.2 3.8 copy-start.29
  22.7 3.7 copy-start.44
  892.2 70.9 %copy-start.32 = (s32[1,2,512]{2,1,0:T(2,128)S(1)}, s32[1,2,512]{2,1,0:T(2,128)}, u32[]{:S(2)}) copy-start(s32[1,2,512]{2,1,0:T(2,128)} %param.19) | copy-start | bytes 12292
  992.1 3.5 copy-start.50
  996.9 124.2 %copy-start.5 = (bf16[1,2,512,512]{3,2,1,0:T(8,128)(2,1)S(1)}, bf16[1,2,512,512]{3,2,1,0:T(8,128)(2,1)}, u32[]{:S(2)}) copy-start(bf16[1,2,512,512]{3,2,1,0:T(8,128)(2,1)} %param.18) | copy-start | bytes 3145732
  996.9 124.2 %copy-start.35 = (f32[512]{0:T(512)S(1)}, f32[512]{0:T(512)}, u32[]{:S(2)}) copy-start(f32[512]{0:T(512)} %param.21) | copy-start | bytes 6148
  996.9 124.2 %copy-start.39 = (f32[2,512]{1,0:T(2,128)S(1)}, f32[2,512]{1,0:T(2,128)}, u32[]{:S(2)}) copy-start(f32[2,512]{1,0:T(2,128)} %get-tuple-element.281) | copy-start | bytes 12292
  998.0 1.3 collective-permute-start
  1046.2 4.0 copy-start.40
  1048.5 417.5 %all-reduce.5.cloned.1.call-start = ((), (), s32[]{:S(2)}) async-start(), calls=%async_computation.2 | async-start | bytes 25165824 | tf_op jit(solution)/shard_map/psum | solution.py:302
  1050.2 72.2 %collective-permute-start.1 = (f32[8,512]{1,0:T(8,128)S(1)}, f32[8,512]{1,0:T(8,128)S(1)}, u32[]{:S(2)}, u32[]{:S(2)}) collective-permute-start(f32[8,512]{1,0:T(8,128)S(1)} %convolution_multiply_fusion.1), channel_id=1, source_target_pairs={{0,16},{16,0},{1,17},{17,1},{2,18},{18,2},{3,19},{19,3},{4,20},{20... | collective-permute-start | bytes 49160 | tf_op jit(solution)/shard_map/ppermute | solution.py:19
  1121.2 1.4 collective-permute-start.2
  1125.4 4.7 copy-start.51
  1130.1 4.5 copy-start.9
  1143.4 3.8 copy-start.7
  1152.0 6.9 copy-start.3
  1153.4 10.6 copy-start.2
  1187.6 6.9 copy-start.3
  1188.9 10.6 copy-start.2
  1224.9 3.4 copy-start.17
  1224.9 3.4 copy-start.23
  1233.4 4.4 copy-start.41
  1233.4 4.4 copy-start.43
  1233.4 4.4 copy-start.45
  1375.8 8.0 copy-start.31
  1375.8 8.4 copy-start.16
  1375.8 8.4 copy-start.27
  1466.1 3.4 copy-start.25
  1466.1 4.4 copy-start.24
  1471.6 3.7 copy-start.20
  (30 other events, 60.8 us)
Sparse Core Ops, SparseCore 0:
  1048.7 72.4 reduce-scatter.1
  1231.9 234.1 all-reduce.4
where the time goes:
time: 1500 us; the launch traced here: 1490 us
  local copies, waits for them, and re-layouts  1130 us (75%)
  waiting for transfers between devices  104 us (7%)
  matrix products  95.6 us (6%)
  blocking collectives  83.3 us (6%)
  other arithmetic  51.3 us (3%)
  between operations  17.1 us (1%)
    gather x2, local copies, waits for them, and re-layouts, shards(): jnp.take(position_table.T, jnp.asarray(bucket_index), axis=1)  937 us
    reduce_scatter x1, waiting for transfers between devices, shards(): lax.psum_scatter(lax.dot_general(similarity_gradient, my_queries, (((0,),...  70.9 us
    unnamed x108, local copies, waits for them, and re-layouts  70.5 us
    rev x1, local copies, waits for them, and re-layouts, diagonal_sums(): flipped = square[:, :, ::-1]  64.2 us
    all_gather x1, blocking collectives, shards(): lax.all_gather(document_vectors, 'rows', axis=0, tiled=True)  45.4 us
    psum x1, blocking collectives, shards(): lax.psum((attention_gain_grad, query_grad, key_grad, value_grad, output_g...  37.9 us
    psum x1, waiting for transfers between devices, shards(): lax.psum((attention_gain_grad, query_grad, key_grad, value_grad, output_g...  32.4 us
  transfers between devices with their start and end apart: 5, of which 4 were waited for; matrix products, arithmetic and copies ran while one was open for 11% of the time, Pallas kernels for 0%

commit v1 on v0

--- a/solution.py
+++ b/solution.py
@@ -300,19 +300,22 @@
     position_grad = jnp.dot(diagonal_sums(score_sum), offset_onehot, precision=MATMUL_PRECISION).T
     closing_terms = loss_part[None]
     summed = lax.psum(
-        (
-            attention_gain_grad,
-            query_grad,
-            key_grad,
-            value_grad,
-            output_grad,
-            position_grad,
-            feedforward_gain_grad,
-            inner_grad,
-            outer_grad,
-            closing_terms,
+        lax.psum(
+            (
+                attention_gain_grad,
+                query_grad,
+                key_grad,
+                value_grad,
+                output_grad,
+                position_grad,
+                feedforward_gain_grad,
+                inner_grad,
+                outer_grad,
+                closing_terms,
+            ),
+            "rows",
         ),
-        ("tower", "rows"),
+        "tower",
     )
     (
         attention_gain_grad,

time: 1500 us -> 1860 us (1.24)
  waiting for transfers between devices: 104 us -> 433 us
  blocking collectives: 83.3 us -> 130 us
    psum x1, waiting for transfers between devices: 32.4 us -> 361 us  [shards(): lax.psum((attention_gain_grad, query_grad, key_grad, value_grad, output_g...]
    psum x0 -> x2, blocking collectives: none -> 42.7 us  [the longest x1 39.5 us: shards(): stat_totals = lax.psum(stat_terms, ('tower', 'rows'))]
  transfers between devices with their start and end apart: 5 -> 6, of which waited for: 4 -> 4; matrix products, arithmetic and copies ran while one was open for 11% -> 9% of each run, Pallas kernels for 0% -> 0%
where the time goes in v1:
time: 1860 us; the launch traced here: 1850 us
  local copies, waits for them, and re-layouts  1120 us (60%)
  waiting for transfers between devices  433 us (23%)
  blocking collectives  130 us (7%)
  matrix products  93.2 us (5%)
  other arithmetic  50.9 us (3%)
    gather x2, local copies, waits for them, and re-layouts, shards(): jnp.take(position_table.T, jnp.asarray(bucket_index), axis=1)  932 us
    psum x1, waiting for transfers between devices, shards(): lax.psum((attention_gain_grad, query_grad, key_grad, value_grad, output_g...  361 us
    reduce_scatter x1, waiting for transfers between devices, shards(): lax.psum_scatter(lax.dot_general(similarity_gradient, my_queries, (((0,),...  70.8 us
    unnamed x108, local copies, waits for them, and re-layouts  66.4 us
    rev x1, local copies, waits for them, and re-layouts, diagonal_sums(): flipped = square[:, :, ::-1]  64.2 us
    all_gather x1, blocking collectives, shards(): lax.all_gather(document_vectors, 'rows', axis=0, tiled=True)  45.4 us
    psum x1, blocking collectives, shards(): lax.psum((attention_gain_grad, query_grad, key_grad, value_grad, output_g...  42.2 us
    psum x1, blocking collectives, shards(): stat_totals = lax.psum(stat_terms, ('tower', 'rows'))  39.5 us
  transfers between devices with their start and end apart: 6, of which 4 were waited for; matrix products, arithmetic and copies ran while one was open for 9% of the time, Pallas kernels for 0%

profile of v1, /device:TPU:0, one launch (start us, length us, event | category | flops | bytes accessed | tf_op | source)
XLA Modules:
  0.0 1850.4 jit_solution(5502386389642978992)
XLA Ops:
  26.5 861.6 %gather_fusion = f32[262144,8]{1,0:T(8,128)} fusion(f32[8,32]{0,1:T(8,128)S(1)} %bitcast.203, s32[262144]{0:T(1024)S(1)} %broadcast_clamp_fusion), kind=kCustom, calls=%fused_computation | custom fusion | bytes 17825792 | tf_op jit(solution)/shard_map/jit(_take)/gather | solution.py:110
  888.1 70.9 %copy.45 = f32[512,512,8]{0,1,2:T(8,128)} copy(f32[512,512,8]{2,1,0:T(8,128)} %bitcast.13) | data formatting | bytes 16777216 | tf_op jit(solution)/shard_map/jit(_take)/gather | solution.py:110
  960.1 23.3 %while.29 = (s32[]{:T(128)}, bf16[2,512,512]{2,1,0:T(8,128)(2,1)}, f32[2,8,512]{2,1,0:T(8,128)S(1)}, bf16[2,512,512]{1,2,0:T(8,128)(2,1)}, s32[2,512]{1,0:T(2,12...) while((s32[]{:T(128)}, bf16[2,512,512]{2,1,0:T(8,128)(2,1)}, ...), condition=%wide.region_4.5_spmd, body=%wide.region_1.0_spmd.sunk | while | flops 554168320 | bytes 41556588 | solution.py:144
  961.6 5.0 fusion.126
  973.0 5.0 fusion.126
  988.4 3.4 fusion.8
  995.6 45.4 %all_gather.3 = f32[256,512]{1,0:T(8,128)S(1)} all-gather(f32[16,512]{1,0:T(8,128)S(1)} %broadcast_select_fusion), channel_id=1, replica_groups=mesh['tower'=2,'rows'=16] {'rows'}, dimensions={0}, use_global_device_ids=true | all-gather | bytes 557056 | tf_op jit(solution)/shard_map/all_gather | solution.py:180
  1046.4 70.8 %reduce-scatter.2.cloned.1.call-done = f32[16,512]{1,0:T(8,128)} async-done(((f32[256,512]{1,0:T(8,128)}), f32[16,512]{1,0:T(8,128)}) %reduce-scatter.2.cloned.1.call-update) | async-done | bytes 32784 | tf_op jit(solution)/shard_map/reduce_scatter | solution.py:208
  1121.0 4.4 fusion.56
  1127.9 4.6 fusion.44
  1142.7 74.3 %while.30 = (s32[]{:T(128)}, f32[8,512,512]{1,2,0:T(8,128)}, bf16[2,512,512]{2,1,0:T(8,128)(2,1)}, bf16[2,512,512]{2,1,0:T(8,128)(2,1)}, bf16[2,512,512]{2,1,0:T...) while((s32[]{:T(128)}, f32[8,512,512]{1,2,0:T(8,128)}, ...), condition=%wide.region_15.16_spmd.clone, body=%wide.region_13.15_spmd.clone.sunk | while | flops 1368387584 | bytes 197745472 | solution.py:279
  1145.3 3.4 constant_dynamic-slice_fusion.22
  1150.9 5.0 multiply_reduce_fusion.7
  1155.9 9.8 select_add_fusion.2
  1167.8 4.8 fusion.140
  1180.9 3.4 constant_dynamic-slice_fusion.22
  1186.5 5.0 multiply_reduce_fusion.7
  1191.4 13.0 select_add_fusion.2
  1206.6 4.8 fusion.140
  1216.9 3.4 fusion.53
  1223.8 360.8 %all-reduce.8.cloned.1.call-done = (f32[512,512]{1,0:T(8,128)}, f32[512,512]{1,0:T(8,128)}, f32[512,512]{1,0:T(8,128)}, f32[512,512]{1,0:T(8,128)}, f32[512,2048]{1,0:T(8,128)}, /*index=5*/f32[2048,512]{1,0:T(8,128)}) async-done(((f32[512,512]{1,0:T(8,128)}, f32[512,512]{1,0:T(8,128)}, f32[512,512]{1,0:T(8,128)}, f32[512,512]{1,0:T(8,128)}, f32[512,2048]{1,0:T(8,128)}, /*index=5*/f32[2048,512]{1,0:T(8,128)}), ...) | async-done | bytes 12582928 | tf_op jit(solution)/shard_map/psum | solution.py:303
  1588.0 39.5 %psum.167 = f32[4]{0:T(128)S(1)} all-reduce(f32[4]{0:T(128)S(1)} %pad_maximum_fusion), channel_id=1, replica_groups=mesh['tower'=2,'rows'=16] {'tower','rows'}, use_global_device_ids=true, to_apply=%region_46.47 | all-reduce | flops 4 | bytes 32 | tf_op jit(solution)/shard_map/psum | solution.py:164
  1630.9 64.2 %rev.6 = f32[8,512,512]{1,2,0:T(8,128)} reverse(f32[8,512,512]{1,2,0:T(8,128)} %get-tuple-element.126), dimensions={2} | reverse | bytes 16777216 | tf_op jit(solution)/shard_map/rev | solution.py:81
  1695.1 9.2 copy.71
  1704.3 11.6 pad_bitcast_fusion
  1715.9 15.2 copy.73
  1731.1 6.0 slice.14
  1737.1 12.5 reshape.408
  1749.7 17.2 reshape.392
  1766.9 7.3 reduce_sum.180
  1780.3 42.2 %all-reduce.1 = (f32[512]{0:T(512)S(1)}, f32[32,8]{0,1:T(8,128)S(1)}, f32[512]{0:T(512)S(1)}, f32[1]{0:T(128)}) all-reduce(f32[512]{0:T(512)S(1)} %get-tuple-element.208, f32[32,8]{0,1:T(8,128)S(1)} %fusion.48, f32[512]{0:T(512)S(1)} %copy-done.45, f32[1]{0:T(128)} %bitcast.27), channel_id=1, replica_groups=mesh['tower'=2,'rows'=16] {'rows'}, use_global_device_ids=true, to_apply=%region_18.19 | all-reduce | flops 1281 | bytes 10248 | tf_op jit(solution)/shard_map/psum | solution.py:303
  1826.4 3.8 fusion.18
  (240 shorter events, 119.6 us)
Async XLA Ops:
  7.2 978.7 %copy-start = (bf16[512,2048]{1,0:T(8,128)(2,1)S(1)}, bf16[512,2048]{1,0:T(8,128)(2,1)}, u32[]{:S(2)}) copy-start(bf16[512,2048]{1,0:T(8,128)(2,1)} %param.28) | copy-start | bytes 6291460
  7.2 1110.0 %reduce-scatter.2.cloned.1.call-start = ((), (), s32[]{:S(2)}) async-start(), calls=%async_computation.1 | async-start | bytes 557056 | tf_op jit(solution)/shard_map/reduce_scatter | solution.py:208
  7.2 3.8 copy-start.29
  22.7 3.7 copy-start.44
  888.0 70.9 %copy-start.32 = (s32[1,2,512]{2,1,0:T(2,128)S(1)}, s32[1,2,512]{2,1,0:T(2,128)}, u32[]{:S(2)}) copy-start(s32[1,2,512]{2,1,0:T(2,128)} %param.19) | copy-start | bytes 12292
  988.3 3.5 copy-start.50
  993.2 124.1 %copy-start.5 = (bf16[1,2,512,512]{3,2,1,0:T(8,128)(2,1)S(1)}, bf16[1,2,512,512]{3,2,1,0:T(8,128)(2,1)}, u32[]{:S(2)}) copy-start(bf16[1,2,512,512]{3,2,1,0:T(8,128)(2,1)} %param.18) | copy-start | bytes 3145732
  993.2 124.1 %copy-start.35 = (f32[512]{0:T(512)S(1)}, f32[512]{0:T(512)}, u32[]{:S(2)}) copy-start(f32[512]{0:T(512)} %param.21) | copy-start | bytes 6148
  993.2 124.1 %copy-start.39 = (f32[2,512]{1,0:T(2,128)S(1)}, f32[2,512]{1,0:T(2,128)}, u32[]{:S(2)}) copy-start(f32[2,512]{1,0:T(2,128)} %get-tuple-element.290) | copy-start | bytes 12292
  994.2 1.3 collective-permute-start
  1042.5 3.9 copy-start.40
  1044.7 540.0 %all-reduce.8.cloned.1.call-start = ((), (), s32[]{:S(2)}) async-start(), calls=%async_computation.2 | async-start | bytes 25165824 | tf_op jit(solution)/shard_map/psum | solution.py:303
  1046.3 72.2 %collective-permute-start.1 = (f32[8,512]{1,0:T(8,128)S(1)}, f32[8,512]{1,0:T(8,128)S(1)}, u32[]{:S(2)}, u32[]{:S(2)}) collective-permute-start(f32[8,512]{1,0:T(8,128)S(1)} %convolution_multiply_fusion.1), channel_id=1, source_target_pairs={{0,16},{16,0},{1,17},{17,1},{2,18},{18,2},{3,19},{19,3},{4,20},{20... | collective-permute-start | bytes 49160 | tf_op jit(solution)/shard_map/ppermute | solution.py:19
  1117.2 1.4 collective-permute-start.2
  1121.0 4.5 copy-start.48
  1144.0 6.9 copy-start.3
  1145.3 10.6 copy-start.2
  1179.5 6.9 copy-start.3
  1180.8 10.6 copy-start.2
  1216.9 3.4 copy-start.17
  1216.9 3.4 copy-start.23
  1223.8 606.4 %all-reduce.10.cloned.1.call-start = ((), (), s32[]{:S(2)}) async-start(), calls=%async_computation.3 | async-start | bytes 25165824 | tf_op jit(solution)/shard_map/psum | solution.py:302
  1584.7 42.8 %copy-start.12 = (f32[1024,512]{1,0:T(8,128)S(1)}, f32[1024,512]{1,0:T(8,128)}, u32[]{:S(2)}) copy-start(f32[1024,512]{1,0:T(8,128)} %copy-done.11) | copy-start | bytes 6291460
  1584.7 45.6 %copy-start.41 = (f32[8]{0:T(128)S(1)}, f32[8]{0:T(128)}, u32[]{:S(2)}) copy-start(f32[8]{0:T(128)} %copy-done.40) | copy-start | bytes 100
  1584.7 45.6 %copy-start.43 = (f32[8]{0:T(128)S(1)}, f32[8]{0:T(128)}, u32[]{:S(2)}) copy-start(f32[8]{0:T(128)} %copy-done.42) | copy-start | bytes 100
  1584.7 45.6 %copy-start.46 = (f32[8]{0:T(128)S(1)}, f32[8]{0:T(128)}, u32[]{:S(2)}) copy-start(f32[8]{0:T(128)} %get-tuple-element.210) | copy-start | bytes 100
  1766.9 8.1 copy-start.31
  1766.9 8.5 copy-start.16
  1766.9 8.5 copy-start.27
  1830.2 3.4 copy-start.25
  1830.2 4.4 copy-start.24
  1835.7 3.7 copy-start.20
  (31 other events, 63.7 us)
Sparse Core Ops, SparseCore 0:
  1044.8 72.3 reduce-scatter.1
  1223.9 360.7 all-reduce.7
  1587.8 49.2 all-reduce.9
